TPU v7x, 32 devices: a whole 2x2x4 slice. The times are simulated.
32 devices in a mesh: rows: 8 (over z, y), cols: 4 (over x, core).
Axes of the slice: x: 2, y: 2, z: 4, core: 2. Of those that a mesh axis runs over, the one named last changes fastest.
Arguments:
- features: bfloat16 [256, 1024], P('cols', 'rows'), may hold values from -6 to 6
- weight_matrix: bfloat16 [256, 256], replicated, may hold values from -0.375 to 0.375
- bias_vector: float32 [256], replicated, may hold values from -3 to 3
- adjacency_tiles: bfloat16 [8, 5, 128, 128], P('rows')
- tile_cols: int32 [8, 5], P('rows'), may hold values from 0 to 7, as said below
- tile_count: int32 [8], P('rows'), may hold values from 3 to 5, as said below
- out_grad: bfloat16 [256, 1024], P('cols', 'rows'), may hold values from -6 to 6
Outputs:
- layer_out: bfloat16 [256, 1024], P('cols', 'rows')
- feature_grad: bfloat16 [256, 1024], P('cols', 'rows')
- weight_grad: float32 [256, 256], P('cols')
- bias_grad: float32 [256], P('cols')
Inputs may be any that keep to these rules, and one draw needn't show every extreme that they name: `tile_cols`: the live slots of a row block name distinct column blocks, its own among them; the pattern is symmetric: c is live in row block b exactly when b is live in row block c, and that tile is the transpose of the one of b in c's list. Slots past tile_count hold the row block's own index. Outside the hub's row, every live column block other than the hub lies within 1 block of the row block around the cycle of 8 blocks; the hub's own row also holds such band blocks. `tile_count`: exactly one row block, the hub, has all 5 slots live.
All inputs are finite; a program needn't handle non-finite values.
Results may differ from a plain program's by a relative error of at most 0.008.
Values may be sent and summed in bfloat16 or wider, within the bound.
A program may use at most 64 MiB of HBM per device.

v0:
```python
import math

import jax
import jax.numpy as jnp
from jax import lax
from jax.sharding import PartitionSpec as P


def block_products(panel_rows, adjacency_tiles, tile_cols, alive_mask):
    feature_width = panel_rows.shape[0]
    tile_side = adjacency_tiles.shape[-1]
    panel_grid = panel_rows.reshape(feature_width, -1, tile_side)
    picked = jnp.take(panel_grid, tile_cols, axis=1)
    picked = jnp.where(alive_mask[None, :, :, None], picked, jnp.zeros((), jnp.bfloat16))
    result = jnp.einsum(
        "fbsk,bsrk->fbr", picked, adjacency_tiles, preferred_element_type=jnp.float32
    )
    return result.reshape(feature_width, -1)


def per_device(
    features, weight_matrix, bias_vector, adjacency_tiles, tile_cols, tile_count, out_grad
):
    feature_width, rows_here = features.shape
    blocks_here, slot_count = tile_cols.shape
    tile_side = adjacency_tiles.shape[-1]
    column_index = lax.axis_index("cols")
    rows_count = lax.axis_size("rows")
    alive_mask = jnp.arange(slot_count, dtype=jnp.int32)[None, :] < tile_count[:, None]
    all_panels = lax.all_gather(features, "rows", axis=1, tiled=True)
    aggregated = block_products(all_panels, adjacency_tiles, tile_cols, alive_mask).astype(
        jnp.bfloat16
    )
    aggregated_full = lax.all_gather(aggregated, "cols", axis=0, tiled=True)
    weight_rows = lax.dynamic_slice_in_dim(
        weight_matrix, column_index * feature_width, feature_width, 0
    )
    bias_rows = lax.dynamic_slice_in_dim(
        bias_vector, column_index * feature_width, feature_width, 0
    )
    preact = (
        jnp.dot(weight_rows, aggregated_full, preferred_element_type=jnp.float32)
        + bias_rows[:, None]
    )
    sigmoid_pre = jax.nn.sigmoid(preact)
    layer_out = (preact * sigmoid_pre).astype(jnp.bfloat16)
    pre_grad = (
        out_grad.astype(jnp.float32) * sigmoid_pre * (1.0 + preact * (1.0 - sigmoid_pre))
    ).astype(jnp.bfloat16)
    partial_grad = jnp.einsum(
        "oi,on->in", weight_rows, pre_grad, preferred_element_type=jnp.float32
    )
    agg_grad = lax.psum_scatter(partial_grad, "cols", scatter_dimension=0, tiled=True).astype(
        jnp.bfloat16
    )
    grad_scale = 1.0 / math.sqrt(rows_here * rows_count)
    weight_part = (
        jnp.einsum("fn,in->fi", pre_grad, aggregated_full, preferred_element_type=jnp.float32)
        * grad_scale
    )
    bias_part = jnp.sum(pre_grad.astype(jnp.float32), axis=1) * grad_scale
    weight_grad, bias_grad = lax.psum((weight_part, bias_part), "rows")
    own_blocks = agg_grad.reshape(feature_width, blocks_here, tile_side)
    contrib_terms = jnp.einsum(
        "fbr,bsrk->bsfk", own_blocks, adjacency_tiles, preferred_element_type=jnp.float32
    )
    contrib_terms = contrib_terms * alive_mask[:, :, None, None].astype(jnp.float32)
    flat_terms = contrib_terms.reshape(-1, feature_width, tile_side)
    row_count = blocks_here * lax.axis_size("rows")
    inside = (tile_cols >= 0) & (tile_cols < row_count)
    target = jnp.where(inside, tile_cols, row_count).reshape(-1)
    empty = jnp.zeros((row_count, feature_width, tile_side), jnp.float32)
    gathered_grad = lax.psum_scatter(
        empty.at[target].add(flat_terms, mode="drop"), "rows", scatter_dimension=0, tiled=True
    )
    feature_grad = (
        gathered_grad.transpose(1, 0, 2).reshape(feature_width, rows_here).astype(jnp.bfloat16)
    )
    return (layer_out, feature_grad, weight_grad, bias_grad)


def solution(mesh):
    return jax.shard_map(
        per_device,
        mesh=mesh,
        in_specs=(
            P("cols", "rows"),
            P(),
            P(),
            P("rows", None, None, None),
            P("rows", None),
            P("rows"),
            P("cols", "rows"),
        ),
        out_specs=(P("cols", "rows"), P("cols", "rows"), P("cols", None), P("cols")),
        check_vma=False,
    )
```

profile of v0, /device:TPU:0, one launch (start us, length us, event | category | flops | bytes accessed | tf_op | source)
XLA Modules:
  0.0 209.7 jit_solution(17363229006679243777)
XLA Ops:
  7.2 0.0 copy-start
  7.2 0.0 copy-start.6
  7.2 0.0 copy-start.2
  7.2 0.0 reduce-scatter.3.cloned.1.call-start
  7.2 0.6 copy-done.6
  8.6 0.0 copy-done.2
  8.6 27.9 %all_gather.6 = bf16[64,1024]{1,0:T(8,128)(2,1)S(1)} all-gather(bf16[64,128]{1,0:T(8,128)(2,1)S(1)} %copy-done.2), channel_id=1, replica_groups=mesh['rows'=8,'cols'=4] {'rows'}, dimensions={1}, use_global_device_ids=true | all-gather | bytes 147456 | tf_op jit(solution)/shard_map/all_gather | solution.py:30
  36.5 0.6 gather_fusion
  37.1 0.0 copy-done
  37.1 0.0 copy-start.3
  37.1 0.2 fusion.2
  37.3 5.4 %all_gather.7 = bf16[256,128]{1,0:T(8,128)(2,1)S(1)} all-gather(bf16[64,128]{1,0:T(8,128)(2,1)S(1)} %fusion.2), channel_id=1, replica_groups=mesh['rows'=8,'cols'=4] {'cols'}, dimensions={0}, use_global_device_ids=true | all-gather | bytes 81920 | tf_op jit(solution)/shard_map/all_gather | solution.py:34
  42.7 0.7 copy-done.5
  43.4 0.1 dynamic_slice.7
  43.5 0.0 copy-done.3
  43.5 0.9 convert_reduce_fusion
  44.3 0.8 fusion.12
  45.2 0.0 reduce-scatter.3.cloned.1.call-update
  45.2 0.0 reduce-scatter.5.cloned.1.call-start
  45.3 19.1 %reduce-scatter.3.cloned.1.call-done = f32[64,128]{1,0:T(8,128)} async-done(((f32[256,128]{1,0:T(8,128)}), f32[64,128]{1,0:T(8,128)}) %reduce-scatter.3.cloned.1.call-update) | async-done | bytes 32784 | tf_op jit(solution)/shard_map/reduce_scatter | solution.py:53
  64.3 0.9 fusion.1
  65.3 0.8 scatter_fusion
  66.1 0.7 copy-done.1
  66.8 0.0 reduce-scatter.5.cloned.1.call-update
  66.8 0.0 all-reduce.2.cloned.1.call-start
  66.8 0.8 convolution_multiply_fusion
  67.6 0.0 all-reduce.2.cloned.1.call-update
  67.7 21.9 %psum.15 = f32[64]{0:T(128)} all-reduce(f32[64]{0:T(128)S(1)} %broadcast_multiply_fusion), channel_id=1, replica_groups=mesh['rows'=8,'cols'=4] {'rows'}, use_global_device_ids=true, to_apply=%region_5.6 | all-reduce | flops 64 | bytes 512 | tf_op jit(solution)/shard_map/psum | solution.py:62
  89.5 40.2 %reduce-scatter.5.cloned.1.call-done = f32[1,64,128]{2,1,0:T(8,128)} async-done(((f32[8,64,128]{2,1,0:T(8,128)}), f32[1,64,128]{2,1,0:T(8,128)}) %reduce-scatter.5.cloned.1.call-update) | async-done | bytes 32784 | tf_op jit(solution)/shard_map/reduce_scatter | solution.py:73
  129.8 1.4 convert_bitcast_fusion
  131.1 70.5 %all-reduce.2.cloned.1.call-done = f32[64,256]{1,0:T(8,128)} async-done(((f32[64,256]{1,0:T(8,128)}), f32[64,256]{1,0:T(8,128)}) %all-reduce.2.cloned.1.call-update) | async-done | bytes 65552 | tf_op jit(solution)/shard_map/psum | solution.py:62
  201.7 1.5 copy.17
  (13 shorter events, 0.1 us)
Async XLA Ops:
  7.2 29.9 %copy-start = (bf16[1,5,128,128]{3,2,1,0:T(8,128)(2,1)S(1)}, bf16[1,5,128,128]{3,2,1,0:T(8,128)(2,1)}, u32[]{:S(2)}) copy-start(bf16[1,5,128,128]{3,2,1,0:T(8,128)(2,1)} %param.10) | copy-start | bytes 491524
  7.2 0.7 copy-start.6
  7.2 1.4 copy-start.2
  7.2 57.1 %reduce-scatter.3.cloned.1.call-start = ((), (), s32[]{:S(2)}) async-start(), calls=%async_computation.2 | async-start | bytes 163840 | tf_op jit(solution)/shard_map/reduce_scatter | solution.py:53
  37.1 6.4 %copy-start.3 = (bf16[256,256]{1,0:T(8,128)(2,1)S(1)}, bf16[256,256]{1,0:T(8,128)(2,1)}, u32[]{:S(2)}) copy-start(bf16[256,256]{1,0:T(8,128)(2,1)} %param.8) | copy-start | bytes 393220
  37.3 6.1 %copy-start.4 = (bf16[64,128]{1,0:T(8,128)(2,1)S(1)}, bf16[64,128]{1,0:T(8,128)(2,1)}, u32[]{:S(2)}) copy-start(bf16[64,128]{1,0:T(8,128)(2,1)} %param.13) | copy-start | bytes 49156
  42.7 0.7 copy-start.5
  45.2 84.6 %reduce-scatter.5.cloned.1.call-start = ((), (), s32[]{:S(2)}) async-start(), calls=%async_computation.3 | async-start | bytes 294912 | tf_op jit(solution)/shard_map/reduce_scatter | solution.py:73
  66.1 0.7 copy-start.1
  66.8 134.9 %all-reduce.2.cloned.1.call-start = ((), (), s32[]{:S(2)}) async-start(), calls=%async_computation.4 | async-start | bytes 131072 | tf_op jit(solution)/shard_map/psum | solution.py:62
Sparse Core Ops, SparseCore 0:
  45.3 18.9 reduce-scatter.2
  68.0 61.6 reduce-scatter.4
  134.1 67.4 all-reduce.1
where the time goes:
time: 210 us
  waiting for transfers between devices  130 us (62%)
  blocking collectives  55.2 us (26%)
  between operations  14.5 us (7%)
  local copies, waits for them, and re-layouts  4.16 us (2%)
  matrix products  3.63 us (2%)
  other arithmetic  2.18 us (1%)
    psum x1, waiting for transfers between devices, per_device(): weight_grad, bias_grad = lax.psum((weight_part, bias_part), 'rows')  70.5 us
    reduce_scatter x1, waiting for transfers between devices, per_device(): lax.psum_scatter(empty.at[target].add(flat_terms, mode='drop'), 'rows', s...  40.2 us
    all_gather x1, blocking collectives, per_device(): all_panels = lax.all_gather(features, 'rows', axis=1, tiled=True)  27.9 us
    psum x1, blocking collectives, per_device(): weight_grad, bias_grad = lax.psum((weight_part, bias_part), 'rows')  21.9 us
    reduce_scatter x1, waiting for transfers between devices, per_device(): lax.psum_scatter(partial_grad, 'cols', scatter_dimension=0, tiled=True)  19.1 us
    all_gather x1, blocking collectives, per_device(): aggregated_full = lax.all_gather(aggregated, 'cols', axis=0, tiled=True)  5.38 us
  transfers between devices with their start and end apart: 3, of which 3 were waited for; matrix products, arithmetic and copies ran while one was open for 1% of the time, Pallas kernels for 0%

commit v1 on v0

v1 whole, which is shorter than its diff:
```python
import functools
import math

import jax
import jax.numpy as jnp
from jax import lax
from jax.experimental import pallas as pl
from jax.experimental.pallas import tpu as pltpu
from jax.sharding import PartitionSpec as P

MESH = pl.DeviceIdType.MESH
NT = (((1,), (1,)), ((), ()))
NN = (((1,), (0,)), ((), ()))


def mm(a, b, dims=NN):
    return lax.dot_general(a, b, dims, preferred_element_type=jnp.float32)


def loop(low, high, body):
    if high - low <= 16:
        for i in range(low, high):
            body(i)
    else:
        pl.loop(low, high)(body)


def kernel(
    nr, nc, scale,
    f_hbm, w_hbm, b_hbm, a_hbm, tc_hbm, tn_hbm, og_hbm,
    lo_out, fg_out, wg_out, bg_out,
    panel, gpan, aggf, ogf, w, wt, bvec, bmat, adj, tc, tn, pg, lo, wpart, rs, wfull, bpart,
    lsem, f_s, f_r, o_s, o_r, a_s, a_r, g_s, g_r, b_s, b_r, w_s, w_r, v_s, v_r,
):
    r, c = lax.axis_index("rows"), lax.axis_index("cols")
    nb, fl, side = panel.shape
    bh, slots = adj.shape[:2]
    chunk = rs.shape[1]
    reducers = fl // chunk

    def row_peer(d):
        return lax.rem(r + d, nr)

    def col_peer(d):
        return lax.rem(c + d, nc)

    local = [
        pltpu.make_async_copy(
            f_hbm.at[:, pl.ds(i * side, side)], panel.at[r * bh + i], lsem.at[7 + i]
        )
        for i in range(bh)
    ]
    mine = pl.ds(pl.multiple_of(c * fl, fl), fl)
    og_local = pltpu.make_async_copy(og_hbm, ogf.at[mine], lsem.at[0])
    w_local = pltpu.make_async_copy(w_hbm, w, lsem.at[1])
    b_local = pltpu.make_async_copy(b_hbm, bvec, lsem.at[2])
    a_local = pltpu.make_async_copy(a_hbm, adj, lsem.at[3])
    tc_local = pltpu.make_async_copy(tc_hbm, tc, lsem.at[4])
    tn_local = pltpu.make_async_copy(tn_hbm, tn, lsem.at[5])
    for cp in local + [og_local, w_local, b_local, tc_local, tn_local, a_local]:
        cp.start()

    barrier = pltpu.get_barrier_semaphore()

    def hello_row(d):
        pl.semaphore_signal(barrier, 1, device_id={"rows": row_peer(d)}, device_id_type=MESH)

    def hello_col(d):
        pl.semaphore_signal(barrier, 1, device_id={"cols": col_peer(d)}, device_id_type=MESH)

    loop(1, nr, hello_row)
    loop(1, nc, hello_col)
    for cp in local:
        cp.wait()
    og_local.wait()
    pl.semaphore_wait(barrier, nr + nc - 2)

    own = pl.ds(r * bh, bh)

    def row_copy(src, dst, s, t, d):
        return pltpu.make_async_remote_copy(
            src_ref=src, dst_ref=dst, send_sem=s.at[d], recv_sem=t.at[d],
            device_id={"rows": row_peer(d)}, device_id_type=MESH,
        )

    def col_copy(src, dst, s, t, d):
        return pltpu.make_async_remote_copy(
            src_ref=src, dst_ref=dst, send_sem=s.at[d], recv_sem=t.at[d],
            device_id={"cols": col_peer(d)}, device_id_type=MESH,
        )

    def f_copy(d):
        return row_copy(panel.at[own], panel.at[own], f_s, f_r, d)

    def o_copy(d):
        return col_copy(ogf.at[mine], ogf.at[mine], o_s, o_r, d)

    def a_copy(d):
        return col_copy(aggf.at[mine], aggf.at[mine], a_s, a_r, d)

    def g_copy(d):
        return row_copy(gpan.at[own], gpan.at[own], g_s, g_r, d)

    def b_copy(d):
        return row_copy(bpart.at[r], bpart.at[r], b_s, b_r, d)

    def w_copy(d):
        src = wpart.at[pl.ds(pl.multiple_of(row_peer(d) * chunk, chunk), chunk)]
        return row_copy(src, rs.at[r], w_s, w_r, d)

    def w_copy_in(d):
        return row_copy(rs.at[r], rs.at[r], w_s, w_r, d)

    my_chunk = pl.ds(pl.multiple_of(r * chunk, chunk), chunk)

    def v_copy(d):
        return row_copy(wfull.at[my_chunk], wfull.at[my_chunk], v_s, v_r, d)

    def v_copy_in(d):
        return row_copy(wfull.at[pl.ds(0, chunk)], wfull.at[pl.ds(0, chunk)], v_s, v_r, d)

    loop(1, nr, lambda d: f_copy(d).start())
    loop(1, nc, lambda d: o_copy(d).start())

    w_local.wait()
    wt[...] = w[...].T
    b_local.wait()
    bmat[...] = jnp.broadcast_to(bvec[...], (side, bvec.shape[1])).T
    tc_local.wait()
    tn_local.wait()
    a_local.wait()

    def products(pan, i):
        def one(s, acc):
            term = mm(pan[tc[i, s]], adj[i, s], NT)
            return acc + jnp.where(s < tn[i], term, 0.0)

        acc = jnp.zeros((fl, side), jnp.float32)
        if slots <= 8:
            for s in range(slots):
                acc = one(s, acc)
            return acc
        return lax.fori_loop(0, slots, one, acc)

    loop(1, nr, lambda d: f_copy(d).wait_recv())
    for i in range(bh):
        aggf[mine, pl.ds(i * side, side)] = products(panel, i).astype(jnp.bfloat16)
    loop(1, nc, lambda d: a_copy(d).start())
    loop(1, nc, lambda d: o_copy(d).wait_recv())
    loop(1, nc, lambda d: a_copy(d).wait_recv())

    for i in range(bh):
        at = pl.ds(i * side, side)
        pre = mm(w[...], aggf[:, at]) + bmat[...]
        sig = jax.nn.sigmoid(pre)
        lo[:, at] = (pre * sig).astype(jnp.bfloat16)
        pg[:, at] = (
            ogf[:, at].astype(jnp.float32) * sig * (1.0 + pre * (1.0 - sig))
        ).astype(jnp.bfloat16)

    wpart[...] = mm(pg[mine, :], aggf[...], NT)

    def w_send(d):
        if reducers == nr:
            w_copy(d).start()
        else:
            pl.when(row_peer(d) < reducers)(lambda: w_copy(d).start())

    loop(1, nr, w_send)
    for i in range(bh):
        gpan[r * bh + i] = mm(wt[mine, :], pg[:, pl.ds(i * side, side)]).astype(jnp.bfloat16)
    loop(1, nr, lambda d: g_copy(d).start())
    ones = jnp.ones((8, bh * side), jnp.bfloat16)
    bpart[r] = mm(ones, pg[mine, :], NT)
    loop(1, nr, lambda d: b_copy(d).start())
    lo_out[...] = lo[mine, :]

    def reduce_chunk():
        loop(1, nr, lambda d: w_copy_in(d).wait_recv())
        rs[r] = wpart[my_chunk, :]
        total = rs[0]
        if nr <= 16:
            for k in range(1, nr):
                total = total + rs[k]
        else:
            total = lax.fori_loop(1, nr, lambda k, t: t + rs[k], total)
        wfull[my_chunk, :] = total * scale
        loop(1, nr, lambda d: v_copy(d).start())

    if reducers == nr:
        reduce_chunk()
    else:
        pl.when(r < reducers)(reduce_chunk)

    loop(1, nr, lambda d: g_copy(d).wait_recv())
    for i in range(bh):
        fg_out[:, pl.ds(i * side, side)] = products(gpan, i).astype(jnp.bfloat16)

    loop(1, nr, lambda d: b_copy(d).wait_recv())
    btot = bpart[0]
    for k in range(1, nr):
        btot = btot + bpart[k]
    bg_out[...] = btot[0:1, :] * scale

    def v_wait(d):
        if reducers == nr:
            v_copy_in(d).wait_recv()
        else:
            pl.when(lax.rem(r - d + nr, nr) < reducers)(lambda: v_copy_in(d).wait_recv())

    loop(1, nr, v_wait)
    wg_out[...] = wfull[...]

    def w_done(d):
        if reducers == nr:
            w_copy(d).wait_send()
        else:
            pl.when(row_peer(d) < reducers)(lambda: w_copy(d).wait_send())

    def v_done(d):
        if reducers == nr:
            v_copy(d).wait_send()
        else:
            pl.when(r < reducers)(lambda: v_copy(d).wait_send())

    loop(1, nr, lambda d: f_copy(d).wait_send())
    loop(1, nc, lambda d: o_copy(d).wait_send())
    loop(1, nc, lambda d: a_copy(d).wait_send())
    loop(1, nr, lambda d: g_copy(d).wait_send())
    loop(1, nr, lambda d: b_copy(d).wait_send())
    loop(1, nr, w_done)
    loop(1, nr, v_done)


def per_device(nr, nc, features, weight_matrix, bias_vector, adjacency_tiles, tile_cols, tile_count, out_grad):
    fl, nodes = features.shape
    bh, slots = tile_cols.shape
    side = adjacency_tiles.shape[-1]
    full = weight_matrix.shape[0]
    nb = bh * nr
    bf, f32 = jnp.bfloat16, jnp.float32
    chunk = max(8, fl // nr)
    scale = 1.0 / math.sqrt(nodes * nr)
    vmem, dma = pltpu.VMEM, pltpu.SemaphoreType.DMA
    any_spec = pl.BlockSpec(memory_space=pl.ANY)
    out_spec = pl.BlockSpec(memory_space=pltpu.VMEM)
    lo, fg, wg, bg = pl.pallas_call(
        functools.partial(kernel, nr, nc, scale),
        out_shape=(
            jax.ShapeDtypeStruct((fl, nodes), bf),
            jax.ShapeDtypeStruct((fl, nodes), bf),
            jax.ShapeDtypeStruct((fl, full), f32),
            jax.ShapeDtypeStruct((1, fl), f32),
        ),
        in_specs=[any_spec] * 7,
        out_specs=(out_spec,) * 4,
        scratch_shapes=[
            vmem((nb, fl, side), bf),
            vmem((nb, fl, side), bf),
            vmem((full, nodes), bf),
            vmem((full, nodes), bf),
            vmem((full, full), bf),
            vmem((full, full), bf),
            vmem((1, full), f32),
            vmem((full, side), f32),
            vmem((bh, slots, side, side), bf),
            pltpu.SMEM((bh, slots), jnp.int32),
            pltpu.SMEM((bh,), jnp.int32),
            vmem((full, nodes), bf),
            vmem((full, nodes), bf),
            vmem((fl, full), f32),
            vmem((nr, chunk, full), f32),
            vmem((fl, full), f32),
            vmem((nr, 8, fl), f32),
            dma((7 + bh,)),
            dma((nr,)), dma((nr,)),
            dma((nc,)), dma((nc,)),
            dma((nc,)), dma((nc,)),
            dma((nr,)), dma((nr,)),
            dma((nr,)), dma((nr,)),
            dma((nr,)), dma((nr,)),
            dma((nr,)), dma((nr,)),
        ],
        compiler_params=pltpu.CompilerParams(
            collective_id=0, has_side_effects=True, vmem_limit_bytes=40 * 1024 * 1024
        ),
    )(
        features, weight_matrix, bias_vector.reshape(1, full), adjacency_tiles,
        tile_cols, tile_count, out_grad,
    )
    return lo, fg, wg, bg.reshape(fl)


def solution(mesh):
    return jax.shard_map(
        functools.partial(per_device, mesh.shape["rows"], mesh.shape["cols"]),
        mesh=mesh,
        in_specs=(
            P("cols", "rows"),
            P(),
            P(),
            P("rows", None, None, None),
            P("rows", None),
            P("rows"),
            P("cols", "rows"),
        ),
        out_specs=(P("cols", "rows"), P("cols", "rows"), P("cols", None), P("cols")),
        check_vma=False,
    )
```

time: 210 us -> 32.2 us (0.15)
  waiting for transfers between devices: 130 us -> 0 us
  blocking collectives: 55.2 us -> 0 us
  Pallas kernels: 0 us -> 24.3 us
  between operations: 14.5 us -> 1.31 us
  matrix products: 3.63 us -> 0 us
  other arithmetic: 2.18 us -> 0 us
  local copies, waits for them, and re-layouts: 4.16 us -> 6.27 us
    psum x1 -> x0, waiting for transfers between devices: 70.5 us -> none  [per_device(): weight_grad, bias_grad = lax.psum((weight_part, bias_part), 'rows')]
    reduce_scatter x2 -> x0, waiting for transfers between devices: 59.3 us -> none  [the longest x1 40.2 us: per_device(): lax.psum_scatter(empty.at[target].add(flat_terms, mode='drop'), 'rows', s...]
    all_gather x2 -> x0, blocking collectives: 33.3 us -> none  [the longest x1 27.9 us: per_device(): all_panels = lax.all_gather(features, 'rows', axis=1, tiled=True)]
    pallas_call x0 -> x1, Pallas kernels: none -> 24.3 us  [per_device(): pl.pallas_call(functools.partial(kernel, nr, nc, scale), out_shape=(jax.S...]
    psum x1 -> x0, blocking collectives: 21.9 us -> none  [per_device(): weight_grad, bias_grad = lax.psum((weight_part, bias_part), 'rows')]
    dot_general x5 -> x0, matrix products: 3.63 us -> none  [the longest x1 0.92 us: per_device(): jnp.einsum('fbr,bsrk->bsfk', own_blocks, adjacency_tiles, preferred_eleme...]
    unnamed x15 -> x16, local copies, waits for them, and re-layouts: 3.48 us -> 6.27 us
  transfers between devices with their start and end apart: 3 -> 0, of which waited for: 3 -> 0; matrix products, arithmetic and copies ran while one was open for 1% -> 0% of each run, Pallas kernels for 0% -> 0%
where the time goes in v1:
time: 32.2 us; the launch traced here: 31.9 us
  Pallas kernels  24.3 us (75%)
  local copies, waits for them, and re-layouts  6.27 us (19%)
  between operations  1.31 us (4%)
    pallas_call x1, Pallas kernels, per_device(): pl.pallas_call(functools.partial(kernel, nr, nc, scale), out_shape=(jax.S...  24.3 us
    unnamed x16, local copies, waits for them, and re-layouts  6.27 us

profile of v1, /device:TPU:0, one launch (start us, length us, event | category | flops | bytes accessed | tf_op | source)
XLA Modules:
  0.0 31.9 jit_solution(16925390904356630891)
XLA Ops:
  1.3 0.0 copy-start.4
  1.3 0.0 copy-start.5
  1.3 0.7 %copy-done.4 = f32[256]{0:T(256)S(1)} copy-done((f32[256]{0:T(256)S(1)}, f32[256]{0:T(256)}, u32[]{:S(2)}) %copy-start.4) | copy-done | bytes 1048
  2.0 0.0 copy-done.5
  2.0 0.0 copy-start
  2.0 0.9 %copy-done = bf16[1,5,128,128]{3,2,1,0:T(8,128)(2,1)S(1)} copy-done((bf16[1,5,128,128]{3,2,1,0:T(8,128)(2,1)S(1)}, bf16[1,5,128,128]{3,2,1,0:T(8,128)(2,1)}, u32[]{:S(2)}) %copy-start) | copy-done | bytes 163864
  2.9 0.0 copy-start.1
  2.9 0.9 %copy-done.1 = bf16[256,256]{1,0:T(8,128)(2,1)S(1)} copy-done((bf16[256,256]{1,0:T(8,128)(2,1)S(1)}, bf16[256,256]{1,0:T(8,128)(2,1)}, u32[]{:S(2)}) %copy-start.1) | copy-done | bytes 131096
  3.8 0.0 copy-start.2
  3.8 0.7 %copy-done.2 = bf16[64,128]{1,0:T(8,128)(2,1)S(1)} copy-done((bf16[64,128]{1,0:T(8,128)(2,1)S(1)}, bf16[64,128]{1,0:T(8,128)(2,1)}, u32[]{:S(2)}) %copy-start.2) | copy-done | bytes 16408
  4.5 0.0 copy-start.3
  4.5 0.7 %copy-done.3 = bf16[64,128]{1,0:T(8,128)(2,1)S(1)} copy-done((bf16[64,128]{1,0:T(8,128)(2,1)S(1)}, bf16[64,128]{1,0:T(8,128)(2,1)}, u32[]{:S(2)}) %copy-start.3) | copy-done | bytes 16408
  5.2 24.3 %shard_map.102 = (bf16[64,128]{1,0:T(8,128)(2,1)S(1)}, bf16[64,128]{1,0:T(8,128)(2,1)S(1)}, f32[64,256]{1,0:T(8,128)S(1)}, f32[1,64]{1,0:T(1,128)S(1)}) custom-call(bf16[64,128]{1,0:T(8,128)(2,1)S(1)} %copy-done.2, bf16[256,256]{1,0:T(8,128)(2,1)S(1)} %copy-done.1, f32[1,256]{1,0:T(1,128)S(1)} %bitcast.2, bf16[1,5,128,128]{3,2,1,0:T(8,128)(2,1)S(1)} %copy-done, ...), custom_call_target="tpu_custom_call" | custom-call | tf_op jit(solution)/shard_map/pallas_call | solution.py:247
  29.5 0.6 %copy.16 = bf16[64,128]{1,0:T(8,128)(2,1)} copy(bf16[64,128]{1,0:T(8,128)(2,1)S(1)} %get-tuple-element.16) | data formatting | bytes 32768
  30.1 0.6 %copy.17 = bf16[64,128]{1,0:T(8,128)(2,1)} copy(bf16[64,128]{1,0:T(8,128)(2,1)S(1)} %get-tuple-element.17) | data formatting | bytes 32768
  30.7 0.6 %copy.18 = f32[64,256]{1,0:T(8,128)} copy(f32[64,256]{1,0:T(8,128)S(1)} %get-tuple-element.18) | data formatting | bytes 131072
  31.4 0.5 %copy.19 = f32[64]{0:T(128)} copy(f32[64]{0:T(128)S(1)} %bitcast.3) | data formatting | bytes 512
Async XLA Ops:
  1.3 0.7 %copy-start.4 = (f32[256]{0:T(256)S(1)}, f32[256]{0:T(256)}, u32[]{:S(2)}) copy-start(f32[256]{0:T(256)} %param.9) | copy-start | bytes 3076
  1.3 0.7 %copy-start.5 = (s32[1,5]{1,0:T(1,128)S(1)}, s32[1,5]{1,0:T(1,128)}, u32[]{:S(2)}) copy-start(s32[1,5]{1,0:T(1,128)} %tc_hbm.1) | copy-start | bytes 64
  2.0 0.9 %copy-start = (bf16[1,5,128,128]{3,2,1,0:T(8,128)(2,1)S(1)}, bf16[1,5,128,128]{3,2,1,0:T(8,128)(2,1)}, u32[]{:S(2)}) copy-start(bf16[1,5,128,128]{3,2,1,0:T(8,128)(2,1)} %a_hbm.1) | copy-start | bytes 491524
  2.9 0.9 %copy-start.1 = (bf16[256,256]{1,0:T(8,128)(2,1)S(1)}, bf16[256,256]{1,0:T(8,128)(2,1)}, u32[]{:S(2)}) copy-start(bf16[256,256]{1,0:T(8,128)(2,1)} %w_hbm.1) | copy-start | bytes 393220
  3.8 0.7 %copy-start.2 = (bf16[64,128]{1,0:T(8,128)(2,1)S(1)}, bf16[64,128]{1,0:T(8,128)(2,1)}, u32[]{:S(2)}) copy-start(bf16[64,128]{1,0:T(8,128)(2,1)} %f_hbm.1) | copy-start | bytes 49156
  4.5 0.7 %copy-start.3 = (bf16[64,128]{1,0:T(8,128)(2,1)S(1)}, bf16[64,128]{1,0:T(8,128)(2,1)}, u32[]{:S(2)}) copy-start(bf16[64,128]{1,0:T(8,128)(2,1)} %og_hbm.1) | copy-start | bytes 49156

commit v2 on v1

--- a/solution.py
+++ b/solution.py
@@ -17,32 +17,65 @@
     return lax.dot_general(a, b, dims, preferred_element_type=jnp.float32)
 
 
+def is_static(count):
+    return count <= 16 and count & (count - 1) == 0
+
+
 def loop(low, high, body):
-    if high - low <= 16:
-        for i in range(low, high):
+    if is_static(high):
+        for i in sorted(range(low, high), key=lambda d: -((d ^ (d >> 1)) + (d & high // 2) * high)):
             body(i)
     else:
         pl.loop(low, high)(body)
+
+
+def partner(me, d, count):
+    if not is_static(count):
+        return lax.rem(me + d, count)
+    other, bit = me, 1
+    while bit < count:
+        if d & bit:
+            other = other + bit - 2 * bit * lax.rem(lax.div(me, bit), 2)
+        bit *= 2
+    return other
+
+
+def stack_halves(x, side):
+    return jnp.concatenate(
+        [x[:, h * side : (h + 1) * side] for h in range(x.shape[1] // side)], axis=0
+    )
 
 
 def kernel(
     nr, nc, scale,
     f_hbm, w_hbm, b_hbm, a_hbm, tc_hbm, tn_hbm, og_hbm,
     lo_out, fg_out, wg_out, bg_out,
-    panel, gpan, aggf, ogf, w, wt, bvec, bmat, adj, tc, tn, pg, lo, wpart, rs, wfull, bpart,
-    lsem, f_s, f_r, o_s, o_r, a_s, a_r, g_s, g_r, b_s, b_r, w_s, w_r, v_s, v_r,
+    panel, gpan, aggf, ogf, w, wt, bvec, bmat, adj, tc, tn, pg, lo, wpart, rs, wfull,
+    lsem, f_s, f_r, o_s, o_r, a_s, a_r, g_s, g_r, w_s, w_r, v_s, v_r,
 ):
     r, c = lax.axis_index("rows"), lax.axis_index("cols")
     nb, fl, side = panel.shape
     bh, slots = adj.shape[:2]
-    chunk = rs.shape[1]
-    reducers = fl // chunk
+    reducers = wpart.shape[0]
+    chunk = fl // reducers
+    parts = w.shape[0] // side
 
     def row_peer(d):
-        return lax.rem(r + d, nr)
+        return partner(r, d, nr)
 
     def col_peer(d):
-        return lax.rem(c + d, nc)
+        return partner(c, d, nc)
+
+    barrier = pltpu.get_barrier_semaphore()
+
+    def hello_row(d):
+        pl.semaphore_signal(barrier, 1, device_id={"rows": row_peer(d)}, device_id_type=MESH)
+
+    def hello_col(d):
+        pl.semaphore_signal(barrier, 1, device_id={"cols": col_peer(d)}, device_id_type=MESH)
+
+    loop(1, nr, hello_row)
+    loop(1, nc, hello_col)
 
     local = [
         pltpu.make_async_copy(
@@ -59,17 +92,6 @@
     tn_local = pltpu.make_async_copy(tn_hbm, tn, lsem.at[5])
     for cp in local + [og_local, w_local, b_local, tc_local, tn_local, a_local]:
         cp.start()
-
-    barrier = pltpu.get_barrier_semaphore()
-
-    def hello_row(d):
-        pl.semaphore_signal(barrier, 1, device_id={"rows": row_peer(d)}, device_id_type=MESH)
-
-    def hello_col(d):
-        pl.semaphore_signal(barrier, 1, device_id={"cols": col_peer(d)}, device_id_type=MESH)
-
-    loop(1, nr, hello_row)
-    loop(1, nc, hello_col)
     for cp in local:
         cp.wait()
     og_local.wait()
@@ -101,23 +123,17 @@
     def g_copy(d):
         return row_copy(gpan.at[own], gpan.at[own], g_s, g_r, d)
 
-    def b_copy(d):
-        return row_copy(bpart.at[r], bpart.at[r], b_s, b_r, d)
-
     def w_copy(d):
-        src = wpart.at[pl.ds(pl.multiple_of(row_peer(d) * chunk, chunk), chunk)]
-        return row_copy(src, rs.at[r], w_s, w_r, d)
+        return row_copy(wpart.at[row_peer(d)], rs.at[r], w_s, w_r, d)
 
     def w_copy_in(d):
         return row_copy(rs.at[r], rs.at[r], w_s, w_r, d)
 
-    my_chunk = pl.ds(pl.multiple_of(r * chunk, chunk), chunk)
-
     def v_copy(d):
-        return row_copy(wfull.at[my_chunk], wfull.at[my_chunk], v_s, v_r, d)
+        return row_copy(wfull.at[r], wfull.at[r], v_s, v_r, d)
 
     def v_copy_in(d):
-        return row_copy(wfull.at[pl.ds(0, chunk)], wfull.at[pl.ds(0, chunk)], v_s, v_r, d)
+        return row_copy(wfull.at[0], wfull.at[0], v_s, v_r, d)
 
     loop(1, nr, lambda d: f_copy(d).start())
     loop(1, nc, lambda d: o_copy(d).start())
@@ -132,7 +148,7 @@
 
     def products(pan, i):
         def one(s, acc):
-            term = mm(pan[tc[i, s]], adj[i, s], NT)
+            term = mm(pan[tc[i, s], pl.ds(0, fl), :], adj[i, s], NT)
             return acc + jnp.where(s < tn[i], term, 0.0)
 
         acc = jnp.zeros((fl, side), jnp.float32)
@@ -158,7 +174,9 @@
             ogf[:, at].astype(jnp.float32) * sig * (1.0 + pre * (1.0 - sig))
         ).astype(jnp.bfloat16)
 
-    wpart[...] = mm(pg[mine, :], aggf[...], NT)
+    wgrad = mm(pg[mine, :], aggf[...], NT)
+    for j in range(reducers):
+        wpart[j] = stack_halves(wgrad[j * chunk : (j + 1) * chunk, :], side).astype(jnp.bfloat16)
 
     def w_send(d):
         if reducers == nr:
@@ -168,23 +186,28 @@
 
     loop(1, nr, w_send)
     for i in range(bh):
-        gpan[r * bh + i] = mm(wt[mine, :], pg[:, pl.ds(i * side, side)]).astype(jnp.bfloat16)
+        at = pl.ds(i * side, side)
+        gpan[r * bh + i, pl.ds(0, fl), :] = mm(wt[mine, :], pg[:, at]).astype(jnp.bfloat16)
+        total = mm(jnp.ones((16, side), jnp.bfloat16), pg[mine, at], NT)
+        high = total.astype(jnp.bfloat16).astype(jnp.float32)
+        middle = (total - high).astype(jnp.bfloat16).astype(jnp.float32)
+        line = lax.broadcasted_iota(jnp.int32, total.shape, 0)
+        rest = jnp.where(line == 2, total - high - middle, 0.0)
+        digits = jnp.where(line == 0, high, jnp.where(line == 1, middle, rest))
+        gpan[r * bh + i, pl.ds(fl, 16), pl.ds(0, fl)] = digits.astype(jnp.bfloat16)
     loop(1, nr, lambda d: g_copy(d).start())
-    ones = jnp.ones((8, bh * side), jnp.bfloat16)
-    bpart[r] = mm(ones, pg[mine, :], NT)
-    loop(1, nr, lambda d: b_copy(d).start())
     lo_out[...] = lo[mine, :]
 
     def reduce_chunk():
         loop(1, nr, lambda d: w_copy_in(d).wait_recv())
-        rs[r] = wpart[my_chunk, :]
-        total = rs[0]
+        rs[r] = wpart[r]
+        total = rs[0].astype(jnp.float32)
         if nr <= 16:
             for k in range(1, nr):
-                total = total + rs[k]
-        else:
-            total = lax.fori_loop(1, nr, lambda k, t: t + rs[k], total)
-        wfull[my_chunk, :] = total * scale
+                total = total + rs[k].astype(jnp.float32)
+        else:
+            total = lax.fori_loop(1, nr, lambda k, t: t + rs[k].astype(jnp.float32), total)
+        wfull[r] = (total * scale).astype(jnp.bfloat16)
         loop(1, nr, lambda d: v_copy(d).start())
 
     if reducers == nr:
@@ -196,11 +219,13 @@
     for i in range(bh):
         fg_out[:, pl.ds(i * side, side)] = products(gpan, i).astype(jnp.bfloat16)
 
-    loop(1, nr, lambda d: b_copy(d).wait_recv())
-    btot = bpart[0]
-    for k in range(1, nr):
-        btot = btot + bpart[k]
-    bg_out[...] = btot[0:1, :] * scale
+    def bias_rows(k):
+        return gpan[k, pl.ds(fl, 16), pl.ds(0, fl)].astype(jnp.float32)
+
+    btot = bias_rows(0)
+    for k in range(1, nb):
+        btot = btot + bias_rows(k)
+    bg_out[...] = jnp.sum(btot, axis=0, keepdims=True) * scale
 
     def v_wait(d):
         if reducers == nr:
@@ -209,7 +234,10 @@
             pl.when(lax.rem(r - d + nr, nr) < reducers)(lambda: v_copy_in(d).wait_recv())
 
     loop(1, nr, v_wait)
-    wg_out[...] = wfull[...]
+    for j in range(reducers):
+        piece = wfull[j].astype(jnp.float32)
+        for h in range(parts):
+            wg_out[pl.ds(j * chunk, chunk), pl.ds(h * side, side)] = piece[h * chunk : (h + 1) * chunk, :]
 
     def w_done(d):
         if reducers == nr:
@@ -227,9 +255,18 @@
     loop(1, nc, lambda d: o_copy(d).wait_send())
     loop(1, nc, lambda d: a_copy(d).wait_send())
     loop(1, nr, lambda d: g_copy(d).wait_send())
-    loop(1, nr, lambda d: b_copy(d).wait_send())
     loop(1, nr, w_done)
     loop(1, nr, v_done)
+
+
+def write_out(*refs):
+    copies = [
+        pltpu.make_async_copy(refs[i], refs[4 + i], refs[8].at[i]) for i in range(4)
+    ]
+    for cp in copies:
+        cp.start()
+    for cp in copies:
+        cp.wait()
 
 
 def per_device(nr, nc, features, weight_matrix, bias_vector, adjacency_tiles, tile_cols, tile_count, out_grad):
@@ -240,23 +277,26 @@
     nb = bh * nr
     bf, f32 = jnp.bfloat16, jnp.float32
     chunk = max(8, fl // nr)
+    piece = (chunk * full // side, side)
     scale = 1.0 / math.sqrt(nodes * nr)
     vmem, dma = pltpu.VMEM, pltpu.SemaphoreType.DMA
+    hbm_spec = pl.BlockSpec(memory_space=pltpu.HBM)
     any_spec = pl.BlockSpec(memory_space=pl.ANY)
     out_spec = pl.BlockSpec(memory_space=pltpu.VMEM)
-    lo, fg, wg, bg = pl.pallas_call(
+    results = (
+        jax.ShapeDtypeStruct((fl, nodes), bf),
+        jax.ShapeDtypeStruct((fl, nodes), bf),
+        jax.ShapeDtypeStruct((fl, full), f32),
+        jax.ShapeDtypeStruct((1, fl), f32),
+    )
+    held = pl.pallas_call(
         functools.partial(kernel, nr, nc, scale),
-        out_shape=(
-            jax.ShapeDtypeStruct((fl, nodes), bf),
-            jax.ShapeDtypeStruct((fl, nodes), bf),
-            jax.ShapeDtypeStruct((fl, full), f32),
-            jax.ShapeDtypeStruct((1, fl), f32),
-        ),
-        in_specs=[any_spec] * 7,
+        out_shape=results,
+        in_specs=[hbm_spec] * 7,
         out_specs=(out_spec,) * 4,
         scratch_shapes=[
             vmem((nb, fl, side), bf),
-            vmem((nb, fl, side), bf),
+            vmem((nb, fl + 16, side), bf),
             vmem((full, nodes), bf),
             vmem((full, nodes), bf),
             vmem((full, full), bf),
@@ -268,10 +308,9 @@
             pltpu.SMEM((bh,), jnp.int32),
             vmem((full, nodes), bf),
             vmem((full, nodes), bf),
-            vmem((fl, full), f32),
-            vmem((nr, chunk, full), f32),
-            vmem((fl, full), f32),
-            vmem((nr, 8, fl), f32),
+            vmem((fl // chunk,) + piece, bf),
+            vmem((nr,) + piece, bf),
+            vmem((fl // chunk,) + piece, bf),
             dma((7 + bh,)),
             dma((nr,)), dma((nr,)),
             dma((nc,)), dma((nc,)),
@@ -279,15 +318,21 @@
             dma((nr,)), dma((nr,)),
             dma((nr,)), dma((nr,)),
             dma((nr,)), dma((nr,)),
-            dma((nr,)), dma((nr,)),
         ],
         compiler_params=pltpu.CompilerParams(
-            collective_id=0, has_side_effects=True, vmem_limit_bytes=40 * 1024 * 1024
+            collective_id=0, has_side_effects=True, vmem_limit_bytes=63 * 1024 * 1024
         ),
     )(
         features, weight_matrix, bias_vector.reshape(1, full), adjacency_tiles,
         tile_cols, tile_count, out_grad,
     )
+    lo, fg, wg, bg = pl.pallas_call(
+        write_out,
+        out_shape=results,
+        in_specs=[out_spec] * 4,
+        out_specs=(hbm_spec,) * 4,
+        scratch_shapes=[dma((4,))], compiler_params=pltpu.CompilerParams(vmem_limit_bytes=63 * 1024 * 1024),
+    )(*held)
     return lo, fg, wg, bg.reshape(fl)
 
 

time: 32.2 us -> 27 us (0.84)
  local copies, waits for them, and re-layouts: 6.27 us -> 0 us
  Pallas kernels: 24.3 us -> 25.4 us
    unnamed x16 -> x0, local copies, waits for them, and re-layouts: 6.27 us -> none
    pallas_call x1 -> x2, Pallas kernels: 24.3 us -> 25.4 us  [the longest x1 23.9 us: per_device(): pl.pallas_call(functools.partial(kernel, nr, nc, scale), out_shape=result...]
where the time goes in v2:
time: 27 us; the launch traced here: 26.7 us
  Pallas kernels  25.4 us (94%)
  between operations  1.29 us (5%)
    pallas_call x1, Pallas kernels, per_device(): pl.pallas_call(functools.partial(kernel, nr, nc, scale), out_shape=result...  23.9 us
    pallas_call x1, Pallas kernels, per_device(): pl.pallas_call(write_out, out_shape=results, in_specs=[out_spec] * 4, out...  1.55 us

profile of v2, /device:TPU:0, one launch (start us, length us, event | category | flops | bytes accessed | tf_op | source)
XLA Modules:
  0.0 26.7 jit_solution(11407332918512116090)
XLA Ops:
  1.3 23.9 %shard_map.102 = (bf16[64,128]{1,0:T(8,128)(2,1)}, bf16[64,128]{1,0:T(8,128)(2,1)}, f32[64,256]{1,0:T(8,128)}, f32[1,64]{1,0:T(1,128)}) custom-call(bf16[64,128]{1,0:T(8,128)(2,1)} %f_hbm.1, bf16[256,256]{1,0:T(8,128)(2,1)} %w_hbm.1, f32[1,256]{1,0:T(1,128)} %bitcast.2, bf16[1,5,128,128]{3,2,1,0:T(8,128)(2,1)} %a_hbm.1, s32[1,5]{1,0:T(1,128)} %tc_hbm.1, ...), custom_call_target="tpu_custom_call" | custom-call | tf_op jit(solution)/shard_map/pallas_call | solution.py:292
  25.1 1.6 %shard_map.103 = (bf16[64,128]{1,0:T(8,128)(2,1)}, bf16[64,128]{1,0:T(8,128)(2,1)}, f32[64,256]{1,0:T(8,128)}, f32[1,64]{1,0:T(1,128)}) custom-call(bf16[64,128]{1,0:T(8,128)(2,1)} %get-tuple-element.12.refs_0_, bf16[64,128]{1,0:T(8,128)(2,1)} %get-tuple-element.13.refs_1_, f32[64,256]{1,0:T(8,128)} %get-tuple-element.14.refs_2_, ...), custom_call_target="tpu_custom_call" | custom-call | tf_op jit(solution)/shard_map/pallas_call | solution.py:329

commit v3 on v2

--- a/solution.py
+++ b/solution.py
@@ -58,7 +58,6 @@
     bh, slots = adj.shape[:2]
     reducers = wpart.shape[0]
     chunk = fl // reducers
-    parts = w.shape[0] // side
 
     def row_peer(d):
         return partner(r, d, nr)
@@ -234,10 +233,7 @@
             pl.when(lax.rem(r - d + nr, nr) < reducers)(lambda: v_copy_in(d).wait_recv())
 
     loop(1, nr, v_wait)
-    for j in range(reducers):
-        piece = wfull[j].astype(jnp.float32)
-        for h in range(parts):
-            wg_out[pl.ds(j * chunk, chunk), pl.ds(h * side, side)] = piece[h * chunk : (h + 1) * chunk, :]
+    wg_out[...] = wfull[...]
 
     def w_done(d):
         if reducers == nr:
@@ -261,10 +257,17 @@
 
 def write_out(*refs):
     copies = [
-        pltpu.make_async_copy(refs[i], refs[4 + i], refs[8].at[i]) for i in range(4)
+        pltpu.make_async_copy(refs[i], refs[4 + i], refs[8].at[i]) for i in (0, 1, 3)
     ]
     for cp in copies:
         cp.start()
+    held, wg_out = refs[2], refs[6]
+    side = held.shape[2]
+    chunk = wg_out.shape[0] // held.shape[0]
+    for j in range(held.shape[0]):
+        piece = held[j].astype(jnp.float32)
+        for h in range(wg_out.shape[1] // side):
+            wg_out[pl.ds(j * chunk, chunk), pl.ds(h * side, side)] = piece[h * chunk : (h + 1) * chunk, :]
     for cp in copies:
         cp.wait()
 
@@ -291,7 +294,7 @@
     )
     held = pl.pallas_call(
         functools.partial(kernel, nr, nc, scale),
-        out_shape=results,
+        out_shape=results[:2] + (jax.ShapeDtypeStruct((fl // chunk,) + piece, bf), results[3]),
         in_specs=[hbm_spec] * 7,
         out_specs=(out_spec,) * 4,
         scratch_shapes=[
@@ -330,7 +333,7 @@
         write_out,
         out_shape=results,
         in_specs=[out_spec] * 4,
-        out_specs=(hbm_spec,) * 4,
+        out_specs=(hbm_spec, hbm_spec, out_spec, hbm_spec),
         scratch_shapes=[dma((4,))], compiler_params=pltpu.CompilerParams(vmem_limit_bytes=63 * 1024 * 1024),
     )(*held)
     return lo, fg, wg, bg.reshape(fl)

time: 27 us -> 27.5 us (1.019)
  Pallas kernels: 25.4 us -> 25.9 us
    pallas_call x1, Pallas kernels: 1.55 us -> 2.07 us  [per_device(): pl.pallas_call(write_out, out_shape=results, in_specs=[out_spec] * 4, out...]
where the time goes in v3:
time: 27.5 us; the launch traced here: 27.2 us
  Pallas kernels  25.9 us (94%)
  between operations  1.29 us (5%)
    pallas_call x1, Pallas kernels, per_device(): pl.pallas_call(functools.partial(kernel, nr, nc, scale), out_shape=result...  23.8 us
    pallas_call x1, Pallas kernels, per_device(): pl.pallas_call(write_out, out_shape=results, in_specs=[out_spec] * 4, out...  2.07 us

profile of v3, /device:TPU:0, one launch (start us, length us, event | category | flops | bytes accessed | tf_op | source)
XLA Modules:
  0.0 27.2 jit_solution(2390683983944742610)
XLA Ops:
  1.3 23.8 %shard_map.102 = (bf16[64,128]{1,0:T(8,128)(2,1)}, bf16[64,128]{1,0:T(8,128)(2,1)}, bf16[8,16,128]{2,1,0:T(8,128)(2,1)}, f32[1,64]{1,0:T(1,128)}) custom-call(bf16[64,128]{1,0:T(8,128)(2,1)} %f_hbm.1, bf16[256,256]{1,0:T(8,128)(2,1)} %w_hbm.1, f32[1,256]{1,0:T(1,128)} %bitcast.2, bf16[1,5,128,128]{3,2,1,0:T(8,128)(2,1)} %a_hbm.1, s32[1,5]{1,0:T(1,128)} %tc_hbm.1, ...), custom_call_target="tpu_custom_call" | custom-call | tf_op jit(solution)/shard_map/pallas_call | solution.py:295
  25.1 2.1 %shard_map.103 = (bf16[64,128]{1,0:T(8,128)(2,1)}, bf16[64,128]{1,0:T(8,128)(2,1)}, f32[64,256]{1,0:T(8,128)}, f32[1,64]{1,0:T(1,128)}) custom-call(bf16[64,128]{1,0:T(8,128)(2,1)} %get-tuple-element.12.refs_0_, bf16[64,128]{1,0:T(8,128)(2,1)} %get-tuple-element.13.refs_1_, bf16[8,16,128]{2,1,0:T(8,128)(2,1)} %get-tuple-element.14.refs_2_, ...), custom_call_target="tpu_custom_call" | custom-call | tf_op jit(solution)/shard_map/pallas_call | solution.py:332
